TPU v7x, 128 devices: a whole 4x4x4 slice. The times are simulated.
128 devices in a mesh: segment: 4 (over z), dp: 32 (over x, y, core).
Axes of the slice: x: 4, y: 4, z: 4, core: 2. Of those that a mesh axis runs over, the one named last changes fastest.
Arguments:
- tokens: float32 [1024, 16, 1536], P('dp', 'segment'), may hold values from -21 to 21
- cotangent: float32 [1024, 16, 1536], P('dp', 'segment'), may hold values from -6 to 6
- image_size: int32 [1024, 2], replicated, may hold values from 4 to 16, as said below
- slot_image: int32 [1024], P('dp'), may hold values from 0 to 1023, each once
- slot_batch: int32 [1024], P('dp'), may hold values from 0 to 3, as said below
- norm_gains: float32 [2, 4, 96], replicated, may hold values from 0.5 to 1.5
- biases: float32 [2, 12, 96], replicated, may hold values from -3 to 3
- depth_taps: float32 [2, 9, 96], replicated, may hold values from -2 to 2
- spread_taps: float32 [2, 4, 96], replicated, may hold values from -4 to 4
- point_first: float32 [2, 96, 96], replicated, may hold values from -0.625 to 0.625
- point_second: float32 [2, 96, 96], replicated, may hold values from -0.625 to 0.625
- mixer_weight: float32 [2, 96, 288], replicated, may hold values from -1.25 to 1.25
- output_weight: float32 [2, 96, 96], replicated, may hold values from -0.625 to 0.625
- expand_weight: float32 [2, 96, 384], replicated, may hold values from -0.625 to 0.625
- expand_bias: float32 [2, 384], replicated, may hold values from -3 to 3
- reduce_weight: float32 [2, 384, 96], replicated, may hold values from -0.3125 to 0.3125
Outputs:
- activations: float32 [1024, 16, 1536], P('dp', 'segment')
- input_grad: float32 [1024, 16, 1536], P('dp', 'segment')
- grad_gains: float32 [2, 4, 96], replicated
- grad_biases: float32 [2, 12, 96], replicated
- grad_depth: float32 [2, 9, 96], replicated
- grad_spread: float32 [2, 4, 96], replicated
- grad_point_first: float32 [2, 96, 96], replicated
- grad_point_second: float32 [2, 96, 96], replicated
- grad_mixer: float32 [2, 96, 288], replicated
- grad_output: float32 [2, 96, 96], replicated
- grad_expand: float32 [2, 96, 384], replicated
- grad_expand_bias: float32 [2, 384], replicated
- grad_reduce: float32 [2, 384, 96], replicated
Inputs may be any that keep to these rules, and one draw needn't show every extreme that they name: `image_size`: heights and widths are even; some image is 16 by 16. `slot_image`: every image sits in exactly one slot. `slot_batch`: the 32 slots of one index of dp hold each micro-batch exactly 8 times.
All inputs are finite; a program needn't handle non-finite values.
Results may differ from a plain program's by a relative error of at most 0.0003.
Values sent between devices are 32-bit elements; how exact they have to be, the bound alone decides.
A program may use at most 320 MiB of HBM per device.

v0:
```python
import functools
import math
from types import SimpleNamespace

import jax
import jax.numpy as jnp
from jax import lax
from jax.experimental import pallas as pl
from jax.experimental.pallas import tpu as pltpu
from jax.sharding import PartitionSpec as P

D = 96
FF = 384
LAYERS = 2
MICRO = 4
SIDE = 16
EPSILON = 1e-05
MASKED_SCORE = -1000000000.0
LANES = 128
TILE = 256
CELLS = SIDE * LANES
DELEGATES = 512
PARAM_ROWS = 32
GRAD_ROWS = 1280
VALUE_PLACES = (768, 864, 1024)
f32 = jnp.float32
bf16 = jnp.bfloat16

NN = (((1,), (0,)), ((), ()))
NT = (((1,), (1,)), ((), ()))
TN = (((0,), (0,)), ((), ()))


def dot(a, b, dims=NN):
    return lax.dot_general(a, b, dims, preferred_element_type=f32)


def halves(v):
    high = v.astype(bf16)
    return high, (v - high.astype(f32)).astype(bf16)


def split(v):
    return jnp.concatenate(halves(v), axis=0)


def mapped(weight_pair, pair):
    both = dot(weight_pair, pair)
    count = both.shape[0] // 2
    return both[:count] + both[count:]


def joined(both):
    count = both.shape[0] // 2
    return both[:count] + both[count:]


def wide(v):
    return jnp.concatenate([v, v], axis=1)


def folded(v):
    return v[:, :LANES] + v[:, LANES:]


def normalized(v):
    centre = v - jnp.sum(v, axis=0, keepdims=True) * (1.0 / D)
    rate = lax.rsqrt(jnp.sum(centre * centre, axis=0, keepdims=True) * (1.0 / D) + EPSILON)
    return centre * rate, rate


def norm_pullback(dn, unit, rate):
    mean = jnp.sum(dn, axis=0, keepdims=True) * (1.0 / D)
    slope = jnp.sum(dn * unit, axis=0, keepdims=True) * (1.0 / D)
    return rate * (dn - mean - unit * slope)


def lane_iota(shape, dim):
    return lax.broadcasted_iota(jnp.int32, shape, dim)


def lane_slot(lane):
    return lane >> 4


def lane_row(lane):
    return lane & 15


def from_row_before(v, lane):
    return jnp.where(lane_row(lane) > 0, pltpu.roll(v, 1, 1), 0.0)


def from_row_after(v, lane):
    return jnp.where(lane_row(lane) < 15, pltpu.roll(v, LANES - 1, 1), 0.0)


def tile_at(j):
    return slice(j * TILE, (j + 1) * TILE)


def padded_tile_at(j):
    return slice(LANES + j * TILE, LANES + (j + 1) * TILE)


def lanes_at(j):
    return slice(j * LANES, (j + 1) * LANES)


def loop(count, body):
    for index in range(count):
        body(index)


def counted(start, stop, body):
    def step(index, carry):
        body(index)
        return carry

    lax.fori_loop(start, stop, step, 0)


def staggered(count, body, gap=1):
    running, index, step = [], 0, 0
    while index < count or running:
        if index < count and step % gap == 0:
            running.append(body(index))
            index += 1
        running = [part for part in running if next(part, "end") != "end"]
        step += 1


def prepare_weights(r, l):
    def left_pair(dst, w):
        n, k = w.shape
        high, low = halves(w)
        dst[0:n, 0:k] = high
        dst[0:n, k : 2 * k] = high
        dst[n : 2 * n, 0:k] = low
        dst[n : 2 * n, k : 2 * k] = low

    for name in ("first", "second", "mixer", "output", "expand"):
        w = getattr(r, name)[l]
        left_pair(getattr(r, name + "_t").at[l], jnp.transpose(w))
        left_pair(getattr(r, name + "_n").at[l], w)
    left_pair(r.reduce_t.at[l], r.reduce[l])
    left_pair(r.reduce_n.at[l], jnp.transpose(r.reduce[l]))
    r.rows[...] = jnp.zeros((PARAM_ROWS, LANES), f32)
    r.rows[0:4, 0:D] = r.gains[l]
    r.rows[4:16, 0:D] = jnp.where(l == 0, r.biases[:, 0], r.biases[:, 1])
    r.rows[16:25, 0:D] = jnp.where(l == 0, r.depth[:, 0], r.depth[:, 1])
    r.rows[25:29, 0:D] = r.spread[l]
    for t in range(3):
        at = slice(t * LANES, (t + 1) * LANES)
        r.rows[29 + t : 30 + t, :] = jnp.where(l == 0, r.ebias[0:1, at], r.ebias[1:2, at])
    columns = jnp.transpose(r.rows[...])
    for k in range(29):
        r.par[l, k] = jnp.broadcast_to(columns[0:D, k : k + 1], (D, LANES))
    for t in range(3):
        r.epar[l, t * LANES : (t + 1) * LANES] = jnp.broadcast_to(
            columns[:, 29 + t : 30 + t], (LANES, LANES)
        )
    lane = lane_iota((D, LANES), 1)
    for b in range(2):
        r.taps[l, b] = jnp.where((lane & 1) == 0, r.par[l, 25 + b], r.par[l, 27 + b])
    r.acc[l] = jnp.zeros((27, D, LANES), f32)
    r.eacc[l] = jnp.zeros((FF, LANES), f32)


def placed(r, slots):
    found = (slots == lane_iota(slots.shape, 0)).astype(f32).astype(bf16)
    per_place = dot(r.by_slot[...].astype(bf16), found)
    return (jnp.broadcast_to(per_place[k : k + 1], (8, slots.shape[1])) for k in range(2))


def one_hots(batch):
    micro = lane_iota((8, LANES), 0)
    upper = ((batch == micro) & (micro < MICRO)).astype(f32)
    lower = ((batch == micro - MICRO) & (micro >= MICRO)).astype(f32)
    return upper, lower


def prepare_rows(r, z):
    lane = lane_iota((8, LANES), 1)
    slot_ids = jnp.zeros((32, LANES), jnp.int32)
    slot_row = lane_iota((32, LANES), 0)
    batch = jnp.zeros((8, LANES), jnp.int32)
    for s in range(32):
        slot_ids = jnp.where(slot_row == s, r.slot_image[s], slot_ids)
        batch = jnp.where((lane >> 2) == s, r.slot_batch[s], batch)
    slot_ids = jnp.concatenate([slot_ids] * 8, axis=1)
    chosen = (slot_ids == lane_iota((32, 1024), 1)).astype(f32).astype(bf16)
    sizes = jnp.concatenate([r.sizes[...].astype(f32), jnp.zeros((6, 1024), f32)], axis=0).astype(bf16)
    r.by_slot[...] = dot(sizes, chosen, NT)
    height, width = placed(r, lane_iota((32, LANES), 1) >> 2)
    count = jnp.where(((lane & 3) + z * 4).astype(f32) < height, width, 0.0)
    r.row_limit[...] = jnp.broadcast_to(jnp.transpose(count)[:, 0:1] * float(D), (LANES, LANES))
    upper, lower = one_hots(batch)
    r.row_onehot[0:8] = upper
    r.row_onehot[8:16] = lower
    r.row_counts[...] = jnp.broadcast_to(jnp.sum(upper * count, axis=1, keepdims=True), (8, LANES))
    for k, kind in enumerate((upper, lower)):
        r.row_columns[k] = jnp.transpose(jnp.concatenate([kind] * 4, axis=0)).astype(bf16)


def prepare_masks(r, z):
    lane = lane_iota((8, LANES), 1)
    batch = jnp.zeros((8, LANES), jnp.int32)
    for s in range(8):
        batch = jnp.where(lane_slot(lane) == s, r.slot_batch[z * 8 + s], batch)
    height, width = placed(r, lane_slot(lane_iota((32, LANES), 1)) + z * 8)
    rows_in = lane_row(lane).astype(f32) < height
    for x in range(SIDE):
        r.mask[:, x * LANES : (x + 1) * LANES] = (rows_in & (width > float(x))).astype(f32)
    r.counts[...] = jnp.where(rows_in, width, 0.0)
    upper, lower = one_hots(batch)
    zero = jnp.zeros((8, 6 * LANES), f32)
    both = jnp.concatenate([upper, lower], axis=1)
    summing = jnp.concatenate([upper] * 3 + [lower] * 3, axis=1)
    r.summing[...] = jnp.concatenate([summing, zero], axis=0).astype(bf16)
    r.placing[...] = jnp.concatenate([both] * 3 + [zero[:, 0:TILE]], axis=0).astype(bf16)
    place = lane_iota((8, DELEGATES), 1)
    height, width = placed(r, (lane_iota((32, DELEGATES), 1) >> 6) + z * 8)
    inside = ((2 * (place & 7)).astype(f32) < height) & ((2 * ((place >> 3) & 7)).astype(f32) < width)
    inside = inside.astype(f32)
    key, query = lane_iota((LANES, LANES), 0), lane_iota((LANES, LANES), 1)
    for p in range(4):
        column = jnp.transpose(inside[:, p * LANES : (p + 1) * LANES])[:, 0:1]
        r.keep[p] = jnp.where((key >> 6) == (query >> 6), jnp.broadcast_to(column, (LANES, LANES)), 0.0)
    lane, place = lane_iota((LANES, DELEGATES), 0), lane_iota((LANES, DELEGATES), 1)
    same = ((place >> 6) == lane_slot(lane)) & ((place & 7) == (lane_row(lane) >> 1))
    for j in range(8):
        r.pool[j * LANES : (j + 1) * LANES] = (
            (same & (((place >> 3) & 7) == j)).astype(f32).astype(bf16)
        )


def take_rows(block, dst, mask):
    for k in range(12):
        at = slice(k * LANES, (k + 1) * LANES)
        rows = jnp.concatenate([block[z, s, :, at] for s in range(8) for z in range(4)], axis=0)
        turned = jnp.transpose(rows)
        for x in range(SIDE):
            lo, hi = max(k * LANES, x * D), min((k + 1) * LANES, (x + 1) * D)
            if lo < hi:
                part = turned[lo - k * LANES : hi - k * LANES]
                dst[lo - x * D : hi - x * D, x * LANES : (x + 1) * LANES] = (
                    part * mask[0:1, x * LANES : (x + 1) * LANES]
                )


def give_rows(src, block):
    for k in range(12):
        parts = []
        for x in range(SIDE):
            lo, hi = max(k * LANES, x * D), min((k + 1) * LANES, (x + 1) * D)
            if lo < hi:
                parts.append(src[lo - x * D : hi - x * D, x * LANES : (x + 1) * LANES])
        turned = jnp.transpose(jnp.concatenate(parts, axis=0))
        for s in range(8):
            for z in range(4):
                place = 4 * (4 * s + z)
                block[z, s, :, k * LANES : (k + 1) * LANES] = turned[place : place + 4]


def three_parts(v, axis=0):
    high, low = halves(v)
    rest = (v - high.astype(f32)) - low.astype(f32)
    return jnp.concatenate([high, low, rest.astype(bf16)], axis=axis)


def lane_sums(upper, lower, r):
    parts = jnp.concatenate([three_parts(upper, 1), three_parts(lower, 1)], axis=1)
    return dot(r.summing[...], parts, NT)[0:8]


def row_mask(r, at):
    lane = (lane_iota((LANES, TILE), 1) + at).astype(f32)
    return lane < wide(r.row_limit[...])


def row_statistics(r):
    upper = jnp.concatenate([r.row_onehot[0:8]] * 3, axis=1).astype(bf16)
    lower = jnp.concatenate([r.row_onehot[8:16]] * 3, axis=1).astype(bf16)

    def body(k):
        at = tile_at(k)
        v = jnp.where(row_mask(r, k * TILE), r.own[:, :, at].reshape(LANES, TILE), 0.0)
        r.row_sums[:, at] = dot(upper, three_parts(v)) + dot(lower, three_parts(v * v))

    loop(6, body)
    total = r.row_sums[:, 0:D]
    for x in range(1, SIDE):
        total = total + r.row_sums[:, x * D : (x + 1) * D]
    return jnp.concatenate([total, r.row_counts[:, 0 : LANES - D]], axis=1)


def corrected_rows(r, out):
    for x in range(SIDE):
        r.row_sums[:, x * D : (x + 1) * D] = r.dstat_rows[:, 0:D]
    zero = jnp.zeros((8, TILE), bf16)

    def body(k):
        at = pl.ds(pl.multiple_of(k * TILE, TILE), TILE)
        parts = jnp.concatenate([three_parts(r.row_sums[:, at]), zero], axis=0)
        dsums, dsquares = dot(r.row_columns[0], parts), dot(r.row_columns[1], parts)
        v = r.rows_in[0, :, :, :, at].reshape(LANES, TILE) + dsums + r.own[:, :, at].reshape(LANES, TILE) * dsquares
        out[:, :, at] = jnp.where(row_mask(r, k * TILE), v, 0.0).reshape(32, 4, TILE)

    counted(0, 6, body)


def statistics_partial(r):
    total = jnp.concatenate([r.sums[0], r.counts[...], jnp.zeros((24, LANES), f32)], axis=0)
    square = jnp.concatenate([r.sums[1], jnp.zeros((32, LANES), f32)], axis=0)
    return lane_sums(total, square, r)


def per_lane(upper, lower, r):
    parts = three_parts(jnp.concatenate([upper, lower], axis=0)).astype(f32)
    turned = jnp.transpose(jnp.concatenate([parts, jnp.zeros((8, LANES), f32)], axis=0)).astype(bf16)
    both = dot(turned, r.placing[...])
    return both[0:D, 0:LANES], both[0:D, LANES:]


def use_statistics(r, l, totals):
    count = totals[0:4, D : D + 1]
    centre = totals[0:4] / count
    variance = totals[4:8] / count - centre * centre
    rate = lax.rsqrt(variance + EPSILON)
    r.stat_rows[l, 0:4] = centre
    r.stat_rows[l, 4:8] = rate
    r.count_rows[...] = jnp.broadcast_to(count, (4, LANES))
    centre_lanes, rate_lanes = per_lane(centre, rate, r)
    r.centre[l] = centre_lanes
    r.rate[l] = rate_lanes


def use_statistics_grad(r, l, totals):
    centre, rate = r.stat_rows[l, 0:4], r.stat_rows[l, 4:8]
    count = r.count_rows[...]
    gain = jnp.concatenate([r.gains[l, 0:1], jnp.zeros((1, LANES - D), f32)], axis=1)
    dcentre = -rate * gain * totals[0:4]
    dvariance = -0.5 * rate * rate * rate * gain * totals[4:8]
    dsums = (dcentre - 2.0 * centre * dvariance) / count
    dsquares = dvariance / count
    r.dstat_rows[0:4] = dsums
    r.dstat_rows[4:8] = 2.0 * dsquares
    if l > 0:
        r.dstat[0], r.dstat[1] = per_lane(dsums, 2.0 * dsquares, r)


def forward_local(r, l):
    r.fmap[l, :, 0:LANES] = jnp.zeros((D, LANES), f32)
    r.fmap[l, :, LANES + CELLS :] = jnp.zeros((D, LANES), f32)

    def body(j):
        v = r.x[l, :, tile_at(j)]
        pair = split((v - wide(r.centre[l])) * wide(r.rate[l] * r.par[l, 0]) + wide(r.par[l, 4]))
        r.n2[l, :, tile_at(j)] = pair
        yield
        out = mapped(r.first_t[l], pair) + wide(r.par[l, 5])
        r.fmap[l, :, padded_tile_at(j)] = out * r.mask[0:1, tile_at(j)]
        yield
        yield
        pair = split(convolved(r, l, j))
        r.d2[l, :, tile_at(j)] = pair
        yield
        out = mapped(r.second_t[l], pair) + wide(r.par[l, 7])
        local = r.x[l, :, tile_at(j)] + out * r.mask[0:1, tile_at(j)]
        r.local[:, tile_at(j)] = local
        unit, rate = normalized(local)
        r.unit1[l, :, tile_at(j)] = unit
        r.rates[l, 0:1, tile_at(j)] = rate
        r.pooled[:, lanes_at(j)] = split(
            0.25 * folded(unit * wide(r.par[l, 1]) + wide(r.par[l, 8]))
        )

    staggered(8, body)


def convolved(r, l, j):
    lane = lane_iota((8, LANES), 1)
    groups = []
    for g in range(12):
        rows = slice(g * 8, (g + 1) * 8)
        taps = [r.par[l, 16 + t, rows, :] for t in range(9)]
        cells = [r.fmap[l, rows, (2 * j + x) * LANES : (2 * j + x + 1) * LANES] for x in range(4)]
        columns = []
        for x in range(2):
            sums = [sum(taps[3 * q + c] * cells[x + c] for c in range(3)) for q in range(3)]
            columns.append(
                r.par[l, 6, rows, :] + sums[1] + from_row_before(sums[0], lane) + from_row_after(sums[2], lane)
            )
        groups.append(jnp.concatenate(columns, axis=1))
    return jnp.concatenate(groups, axis=0)


def forward_mixer(r, l):
    forward_queries(r, l)
    forward_attention(r, l)
    forward_spread(r, l)


def forward_queries(r, l):
    delegates = joined(dot(r.pooled[...], r.pool[...]))
    pair = split(delegates)
    r.g2[l] = pair
    qkv = mapped(r.mixer_t[l], pair)
    queries, keys, values = qkv[0:D], qkv[D : 2 * D], qkv[2 * D :]
    for t in range(4):
        at = slice(t * LANES, (t + 1) * LANES)
        r.qkv[l, 0:D, at] = (queries[:, at] + r.par[l, 9]) * SCALE
        r.qkv[l, D : 2 * D, at] = keys[:, at]
        r.qkv[l, 2 * D :, at] = values[:, at] + r.par[l, 10]


def by_head(v):
    zero = jnp.zeros((HEAD, LANES), f32)
    return jnp.concatenate(
        [jnp.concatenate([v[0:HEAD], zero], axis=1), jnp.concatenate([zero, v[HEAD:]], axis=1)], axis=0
    )


def own_head(v):
    return jnp.concatenate([v[0:HEAD, 0:LANES], v[HEAD:, LANES:]], axis=0)


def left_rows(v):
    turned = jnp.transpose(jnp.concatenate([v, v], axis=0))
    return jnp.concatenate(halves(turned), axis=0)


def left_columns(v):
    high, low = halves(v)
    return jnp.concatenate(
        [jnp.concatenate([high, high], axis=1), jnp.concatenate([low, low], axis=1)], axis=0
    )


def column_product(a_pair, b_pair):
    both = joined(dot(a_pair, b_pair, NT))
    return folded(both)


HEAD = D // 2
SCALE = 1.0 / math.sqrt(HEAD)


def forward_attention(r, l):
    def body(p):
        at = slice(p * LANES, (p + 1) * LANES)
        q, k, v = (r.qkv[l, part * D : (part + 1) * D, at] for part in range(3))
        left, right = left_rows(k), split(by_head(q))
        yield
        scores = joined(dot(left, right))
        scores = jnp.where(wide(r.keep[p]) > 0.0, scores, MASKED_SCORE)
        yield
        weights = jnp.exp(scores - jnp.max(scores, axis=0, keepdims=True))
        probs = weights / jnp.sum(weights, axis=0, keepdims=True)
        r.probs[l, p] = probs
        yield
        r.mixture[:, at] = own_head(mapped(left_columns(v), split(probs)))

    staggered(4, body)


def forward_spread(r, l):
    r.mix2[...] = split(r.mixture[...])

    def spread(t):
        r.up[l, :, tile_at(t)] = joined(dot(r.mix2[...], r.pool[tile_at(t), :], NT))

    loop(4, spread)


def rest_forward(r, l, j):
    mask = r.mask[0:1, tile_at(j)]
    up = r.up[l, :, lanes_at(j)]
    spread = jnp.concatenate([up * r.taps[l, 0], up * r.taps[l, 1]], axis=1) + wide(r.par[l, 11])
    unit2, rate2 = normalized(spread)
    pair = split(unit2 * wide(r.par[l, 2]) + wide(r.par[l, 12]))
    r.s2[l, :, tile_at(j)] = pair
    yield
    middle = r.local[:, tile_at(j)] + mask * (mapped(r.output_t[l], pair) + wide(r.par[l, 13]))
    unit3, rate3 = normalized(middle)
    pair = split(unit3 * wide(r.par[l, 3]) + wide(r.par[l, 14]))
    r.e2[l, :, tile_at(j)] = pair
    yield
    before = mapped(r.expand_t[l], pair) + wide(r.epar[l])
    yield
    normal = 0.5 + 0.5 * lax.erf(before * math.sqrt(0.5))
    slope = normal + before * (jnp.exp(-0.5 * before * before) * (1.0 / math.sqrt(2.0 * math.pi)))
    hidden = split(before * normal)
    r.h2[l, :, tile_at(j)] = hidden
    yield
    out = middle + mask * (mapped(r.reduce_t[l], hidden) + wide(r.par[l, 15]))
    return out, unit2, rate2, unit3, rate3, slope


def rest_backward(r, l, j, dy, unit2, rate2, unit3, rate3, slope):
    def add(k, v):
        r.acc[l, k] += folded(v)

    pair = split(dy)
    r.dy2[:, tile_at(j)] = pair
    add(15, dy)
    yield
    dbefore = mapped(r.reduce_n[l], pair) * slope
    r.eacc[l] += folded(dbefore)
    pair = split(dbefore)
    r.dp2[:, tile_at(j)] = pair
    yield
    de = mapped(r.expand_n[l], pair)
    add(14, de)
    add(3, de * unit3)
    dmiddle = dy + norm_pullback(de * wide(r.par[l, 3]), unit3, rate3)
    r.local[:, tile_at(j)] = dmiddle
    add(13, dmiddle)
    pair = split(dmiddle)
    r.dm2[:, tile_at(j)] = pair
    yield
    ds = mapped(r.output_n[l], pair)
    add(12, ds)
    add(2, ds * unit2)
    dspread = norm_pullback(ds * wide(r.par[l, 2]), unit2, rate2)
    add(11, dspread)
    up = r.up[l, :, lanes_at(j)]
    r.acc[l, 25] += dspread[:, :LANES] * up
    r.acc[l, 26] += dspread[:, LANES:] * up
    r.pooled[:, lanes_at(j)] = split(
        dspread[:, :LANES] * r.taps[l, 0] + dspread[:, LANES:] * r.taps[l, 1]
    )


def forward_rest(r, l):
    def body(j):
        out, unit2, rate2, unit3, rate3, slope = yield from rest_forward(r, l, j)
        r.unit2[:, tile_at(j)] = unit2
        r.unit3[:, tile_at(j)] = unit3
        r.rates2[0:1, tile_at(j)] = rate2
        r.rates2[1:2, tile_at(j)] = rate3
        r.slope[:, tile_at(j)] = slope
        r.x[l + 1, :, tile_at(j)] = out
        r.sums[0] += folded(out)
        r.sums[1] += folded(out * out)

    r.sums[...] = jnp.zeros_like(r.sums)
    staggered(8, body)


def backward_rest(r, l):
    def body(j):
        yield from rest_backward(
            r, l, j, r.dy[:, tile_at(j)], r.unit2[:, tile_at(j)], r.rates2[0:1, tile_at(j)],
            r.unit3[:, tile_at(j)], r.rates2[1:2, tile_at(j)], r.slope[:, tile_at(j)],
        )

    staggered(8, body)


def turn_rest(r, l):
    def body(j):
        out, *kept = yield from rest_forward(r, l, j)
        r.temp[:, tile_at(j)] = out
        yield from rest_backward(r, l, j, r.dy[:, tile_at(j)], *kept)

    staggered(8, body)


def backward_mixer(r, l):
    backward_gather(r, l)
    backward_attention(r, l)
    backward_queries(r, l)
    backward_spread(r, l)


def backward_gather(r, l):
    r.mixture[...] = joined(dot(r.pooled[...], r.pool[...]))


def backward_attention(r, l):
    def body(p):
        at = slice(p * LANES, (p + 1) * LANES)
        q, k, v = (r.qkv[l, part * D : (part + 1) * D, at] for part in range(3))
        probs = r.probs[l, p]
        dout = split(by_head(r.mixture[:, at]))
        left = left_rows(v)
        yield
        dprobs = joined(dot(left, dout))
        yield
        dscores = split(probs * (dprobs - jnp.sum(probs * dprobs, axis=0, keepdims=True)))
        r.dqkv[2 * D :, at] = column_product(dout, split(probs))
        yield
        r.dqkv[0:D, at] = own_head(mapped(left_columns(k), dscores)) * SCALE
        r.dqkv[D : 2 * D, at] = column_product(split(by_head(q)), dscores)

    staggered(4, body)


def backward_queries(r, l):
    dqkv = r.dqkv[...]
    for t in range(4):
        at = slice(t * LANES, (t + 1) * LANES)
        r.acc[l, 9] += dqkv[0:D, at]
        r.acc[l, 10] += dqkv[2 * D :, at]
    pair = split(dqkv)
    r.dq2[...] = pair
    r.mix2[...] = split(mapped(r.mixer_n[l], pair))


def backward_spread(r, l):
    def spread(t):
        r.dup[:, tile_at(t)] = 0.25 * joined(dot(r.mix2[...], r.pool[tile_at(t), :], NT))

    loop(4, spread)


def shifted_maps(r):
    return r.dy, r.dmap.at[0], r.dmap.at[1]


def backward_local(r, l):
    lane = lane_iota((D, LANES), 1)
    for shifted in shifted_maps(r):
        shifted[:, 0:LANES] = jnp.zeros((D, LANES), f32)
        shifted[:, LANES + CELLS :] = jnp.zeros((D, LANES), f32)

    def add(k, v):
        r.acc[l, k] += folded(v)

    def body(j):
        dup = wide(r.dup[:, lanes_at(j)])
        unit = r.unit1[l, :, tile_at(j)]
        add(8, dup)
        add(1, dup * unit)
        dlocal = r.local[:, tile_at(j)] + norm_pullback(
            dup * wide(r.par[l, 1]), unit, r.rates[l, 0:1, tile_at(j)]
        )
        r.local[:, tile_at(j)] = dlocal
        add(7, dlocal)
        pair = split(dlocal)
        r.dl2[:, tile_at(j)] = pair
        yield
        out = mapped(r.second_n[l], pair)
        add(6, out)
        after, same, before = shifted_maps(r)
        same[:, padded_tile_at(j)] = out
        for x in range(2):
            column = out[:, x * LANES : (x + 1) * LANES]
            place = slice((2 * j + x + 1) * LANES, (2 * j + x + 2) * LANES)
            after[:, place] = from_row_after(column, lane)
            before[:, place] = from_row_before(column, lane)
        yield
        yield
        v = convolved_back(r, l, j) * r.mask[0:1, tile_at(j)]
        add(5, v)
        pair = split(v)
        r.df2[:, tile_at(j)] = pair
        yield
        dnormed = mapped(r.first_n[l], pair)
        r.temp[:, tile_at(j)] = dnormed
        r.acc[l, 4] += folded(dnormed)
        r.acc[l, 0] += folded(dnormed * (r.x[l, :, tile_at(j)] - wide(r.centre[l])))

    staggered(8, body)


def convolved_back(r, l, j):
    groups = []
    for g in range(12):
        rows = slice(g * 8, (g + 1) * 8)
        value = [r.fmap[l, rows, (2 * j + x + 1) * LANES : (2 * j + x + 2) * LANES] for x in range(2)]
        columns = [0.0, 0.0]
        for q, shifted in enumerate(shifted_maps(r)):
            source = [shifted[rows, (2 * j + x) * LANES : (2 * j + x + 1) * LANES] for x in range(4)]
            for c in range(3):
                tap = r.par[l, 16 + 3 * q + c, rows, :]
                for x in range(2):
                    columns[x] = columns[x] + tap * source[x + 2 - c]
                r.acc[l, 16 + 3 * q + c, rows, :] += sum(source[x + 2 - c] * value[x] for x in range(2))
        groups.append(jnp.concatenate(columns, axis=1))
    return jnp.concatenate(groups, axis=0)


def statistics_grad_partial(r, l):
    pad = jnp.zeros((LANES - D, LANES), f32)
    return lane_sums(
        jnp.concatenate([r.acc[l, 4], pad], axis=0), jnp.concatenate([r.acc[l, 0], pad], axis=0), r
    )


def backward_input(r, l):
    def body(j):
        v = r.x[l, :, tile_at(j)]
        r.dy[:, tile_at(j)] = (
            r.temp[:, tile_at(j)] * wide(r.rate[l] * r.par[l, 0])
            + r.local[:, tile_at(j)]
            + r.mask[0:1, tile_at(j)] * (wide(r.dstat[0]) + v * wide(r.dstat[1]))
        )

    loop(8, body)


def partial_input(r, l):
    def body(j):
        r.dy[:, tile_at(j)] = (
            r.temp[:, tile_at(j)] * wide(r.rate[l] * r.par[l, 0]) + r.local[:, tile_at(j)]
        )

    loop(8, body)


def big_product(r, l, a, b, place):
    both = joined(dot(a, b, NT))
    both = both[:, 0:D] + both[:, D:]
    for t in range(3):
        r.grads[l, place + t * D : place + (t + 1) * D] = jnp.transpose(both[t * LANES : (t + 1) * LANES])


def small_product(a, b):
    both = joined(dot(a, b, NT))
    return both[:, 0:D] + both[:, D:]


def feed_forward_grads(r, l):
    big_product(r, l, r.dp2[...], r.e2[l], 0)
    big_product(r, l, r.h2[l], r.dy2[...], 288)
    r.grads[l, 576:672, 0:D] = small_product(r.s2[l], r.dm2[...])


def mixer_grads(r, l):
    queries, keys, values = (
        small_product(
            r.g2[l], jnp.concatenate([r.dq2[t * D : (t + 1) * D], r.dq2[(3 + t) * D : (4 + t) * D]], axis=0)
        )
        for t in range(3)
    )
    r.grads[l, 768:864, 0:D] = queries
    r.grads[l, 864:960, 0:D] = keys
    for t, place in enumerate(VALUE_PLACES):
        r.grads[l, place : place + D, D:] = values[:, t * 32 : (t + 1) * 32]


def local_grads(r, l):
    r.grads[l, 1024:1120, 0:D] = small_product(r.n2[l], r.df2[...])
    r.grads[l, 1120:1216, 0:D] = small_product(r.d2[l], r.dl2[...])


def vector_grads(r, l):
    r.acc[l, 0] = r.acc[l, 0] * r.rate[l]
    ones = jnp.ones((8, TILE), f32)
    even = ((lane_iota((8, TILE), 1) & 1) == 0).astype(f32)
    odd = (ones - even).astype(bf16)
    ones, even = ones.astype(bf16), even.astype(bf16)

    def row(kind, v, place, count):
        total = dot(kind, jnp.concatenate(halves(v), axis=1), NT)
        r.grads[l, 1216 + place : 1217 + place, 0:count] = total[0:1]

    for k in range(25):
        row(ones, r.acc[l, k], k, D)
    for b in range(2):
        row(even, r.acc[l, 25 + b], 25 + b, D)
        row(odd, r.acc[l, 25 + b], 27 + b, D)
    for t in range(3):
        row(ones, r.eacc[l, t * LANES : (t + 1) * LANES], 29 + t, LANES)


def weight_grads(r, l):
    feed_forward_grads(r, l)
    mixer_grads(r, l)
    local_grads(r, l)
    vector_grads(r, l)


def scratch_list():
    L = LAYERS
    v = pltpu.VMEM
    return [
        ("first_t", v((L, 192, 192), bf16)),
        ("first_n", v((L, 192, 192), bf16)),
        ("second_t", v((L, 192, 192), bf16)),
        ("second_n", v((L, 192, 192), bf16)),
        ("mixer_t", v((L, 576, 192), bf16)),
        ("mixer_n", v((L, 192, 576), bf16)),
        ("output_t", v((L, 192, 192), bf16)),
        ("output_n", v((L, 192, 192), bf16)),
        ("expand_t", v((L, 768, 192), bf16)),
        ("expand_n", v((L, 192, 768), bf16)),
        ("reduce_t", v((L, 192, 768), bf16)),
        ("reduce_n", v((L, 768, 192), bf16)),
        ("rows", v((PARAM_ROWS, LANES), f32)),
        ("par", v((L, 29, D, LANES), f32)),
        ("epar", v((L, FF, LANES), f32)),
        ("taps", v((L, 2, D, LANES), f32)),
        ("acc", v((L, 27, D, LANES), f32)),
        ("eacc", v((L, FF, LANES), f32)),
        ("mask", v((8, CELLS), f32)),
        ("counts", v((8, LANES), f32)),
        ("summing", v((16, 6 * LANES), bf16)),
        ("placing", v((32, TILE), bf16)),
        ("keep", v((4, LANES, LANES), f32)),
        ("pool", v((8 * LANES, DELEGATES), bf16)),
        ("sums", v((2, D, LANES), f32)),
        ("own", v((32, 4, SIDE * D), f32)),
        ("by_slot", v((8, 32), f32)),
        ("row_limit", v((LANES, LANES), f32)),
        ("row_onehot", v((16, LANES), f32)),
        ("row_counts", v((8, LANES), f32)),
        ("row_columns", v((2, LANES, 32), bf16)),
        ("row_sums", v((8, SIDE * D), f32)),
        ("dstat_rows", v((8, LANES), f32)),
        ("stat_rows", v((L, 8, LANES), f32)),
        ("count_rows", v((4, LANES), f32)),
        ("centre", v((L, D, LANES), f32)),
        ("rate", v((L, D, LANES), f32)),
        ("dstat", v((2, D, LANES), f32)),
        ("x", v((L, D, CELLS), f32)),
        ("n2", v((L, 2 * D, CELLS), bf16)),
        ("fmap", v((L, D, CELLS + 2 * LANES), f32)),
        ("temp", v((D, CELLS), f32)),
        ("d2", v((L, 2 * D, CELLS), bf16)),
        ("local", v((D, CELLS), f32)),
        ("unit1", v((L, D, CELLS), f32)),
        ("rates", v((L, 1, CELLS), f32)),
        ("pooled", v((2 * D, 8 * LANES), bf16)),
        ("g2", v((L, 2 * D, DELEGATES), bf16)),
        ("qkv", v((L, 3 * D, DELEGATES), f32)),
        ("probs", v((L, 4, LANES, TILE), f32)),
        ("mixture", v((D, DELEGATES), f32)),
        ("mix2", v((2 * D, DELEGATES), bf16)),
        ("up", v((L, D, 8 * LANES), f32)),
        ("unit2", v((D, CELLS), f32)),
        ("s2", v((L, 2 * D, CELLS), bf16)),
        ("unit3", v((D, CELLS), f32)),
        ("rates2", v((8, CELLS), f32)),
        ("e2", v((L, 2 * D, CELLS), bf16)),
        ("slope", v((FF, CELLS), f32)),
        ("h2", v((L, 2 * FF, CELLS), bf16)),
        ("dy", v((D, CELLS + 2 * LANES), f32)),
        ("dy2", v((2 * D, CELLS), bf16)),
        ("dp2", v((2 * FF, CELLS), bf16)),
        ("dm2", v((2 * D, CELLS), bf16)),
        ("dqkv", v((3 * D, DELEGATES), f32)),
        ("dq2", v((6 * D, DELEGATES), bf16)),
        ("dup", v((D, 8 * LANES), f32)),
        ("dl2", v((2 * D, CELLS), bf16)),
        ("dmap", v((2, D, CELLS + 2 * LANES), f32)),
        ("df2", v((2 * D, CELLS), bf16)),
        ("grads", v((L, GRAD_ROWS, LANES), f32)),
    ]


PARAMS = (
    "gains", "biases", "depth", "spread", "first", "second", "mixer", "output", "expand", "ebias", "reduce",
)

OTHERS = 15
GROUP = 7
PARCELS = ((0, 0, 1024), (1, 0, 1280), (0, 1024, 256))


class Place:
    def __init__(self):
        dp = lax.axis_index("dp")
        self.z = lax.axis_index("segment")
        self.core = lax.rem(dp, 2)
        self.chip = lax.div(dp, 2)
        self.member = self.z * 2 + self.core

    def chip_at(self, d):
        step = lax.rem(d + 8, 15) + 1
        x, y = lax.div(self.chip, 4) + lax.div(step, 4), lax.rem(self.chip, 4) + lax.rem(step, 4)
        return lax.rem(x, 4) * 4 + lax.rem(y, 4)

    def chip_after(self, d):
        return (self.z, self.chip_at(d) * 2 + self.core)

    def member_after(self, d):
        member = lax.rem(self.member + d, 8)
        return (lax.div(member, 2), self.chip * 2 + lax.rem(member, 2))

    def z_after(self, d):
        return (lax.rem(self.z + d, 4), self.chip * 2 + self.core)

    def sibling(self):
        return (self.z, self.chip * 2 + 1 - self.core)


def remote(src, dst, sends, receives, index, device):
    return pltpu.make_async_remote_copy(
        src_ref=src,
        dst_ref=dst,
        send_sem=sends.at[index],
        recv_sem=receives.at[index],
        device_id=device,
        device_id_type=pl.DeviceIdType.MESH,
    )


def greet(me):
    barrier = pltpu.get_barrier_semaphore()


    def signal(device):
        pl.semaphore_signal(barrier, inc=1, device_id=device, device_id_type=pl.DeviceIdType.MESH)

    counted(1, 16, lambda d: signal(me.chip_after(d)))
    counted(1, 8, lambda d: signal(me.member_after(d)))
    return barrier


class Exchange:
    def __init__(self, count, make, urgent=False):
        self.count, self.make, self.urgent = count, make, urgent

    def each(self, act):
        if self.urgent:
            for d in range(1, self.count + 1):
                act(self.make(d))
        else:
            counted(1, self.count + 1, lambda d: act(self.make(d)))

    def start(self):
        self.each(lambda copy: copy.start())

    def wait(self):
        self.each(lambda copy: copy.wait())


class RowsIn:
    def __init__(self, r, me, src, dst, number):
        self.own = pltpu.make_async_copy(src.at[pl.ds(me.z * 8, 8)], dst.at[me.z], r.row_own.at[number])
        self.copies = [
            remote(
                src.at[pl.ds(lax.rem(me.z + d, 4) * 8, 8)], dst.at[me.z],
                r.row_send, r.row_recv, (number, d), me.z_after(d),
            )
            for d in range(1, 4)
        ]

    def start(self):
        for copy in self.copies:
            copy.start()
        self.own.start()

    def wait(self):
        self.own.wait()
        for copy in self.copies:
            copy.wait()


class RowsOut(RowsIn):
    def __init__(self, r, me, src, dst, number):
        self.own = pltpu.make_async_copy(src.at[me.z], dst, r.row_own.at[number])
        self.copies = [
            remote(
                src.at[lax.rem(me.z + d, 4)], dst,
                r.row_send, r.row_recv, (number, d), me.z_after(d),
            )
            for d in range(1, 4)
        ]


class SmallSum:
    def __init__(self, r, me, number):
        self.r, self.me, self.number = r, me, number
        mine = r.chip_parts.at[number, me.chip]
        self.first = Exchange(
            OTHERS,
            lambda d: remote(mine, mine, r.chip_send, r.chip_recv, (number, d), me.chip_after(d)),
            number in (1, 2),
        )
        group = r.group_parts.at[number, me.member]
        self.second = Exchange(
            GROUP,
            lambda d: remote(group, group, r.group_send, r.group_recv, (number, d), me.member_after(d)),
            number in (1, 2),
        )

    def put(self, value):
        self.r.chip_parts[self.number, self.me.chip] = value

    def start(self):
        self.first.start()

    def step(self):
        self.first.wait()
        total = self.r.chip_parts[self.number, 0]
        for k in range(1, 16):
            total = total + self.r.chip_parts[self.number, k]
        self.r.group_parts[self.number, self.me.member] = total
        self.second.start()

    def finish(self):
        self.second.wait()
        total = self.r.group_parts[self.number, 0]
        for k in range(1, 8):
            total = total + self.r.group_parts[self.number, k]
        return total


class WeightSum:
    def __init__(self, r, me, number):
        self.r, self.me, self.number = r, me, number
        layer, start, rows = PARCELS[number]
        count, size = rows // 2, rows // 32
        grads, totals = r.grads.at[layer], r.totals.at[layer]
        self.half, self.parts, self.planes = (
            getattr(r, kind + str(number)) for kind in ("half", "parts", "planes")
        )

        def half_of(core):
            return pl.ds(pl.multiple_of(start + core * count, 8), count)

        def piece_of(chip):
            return pl.ds(pl.multiple_of(chip * size, 8), size)

        self.mine = grads.at[half_of(me.core)]
        self.own_piece = self.half.at[piece_of(me.chip)]
        self.halves = remote(
            grads.at[half_of(1 - me.core)], self.half, r.half_send, r.half_recv, (number, 0), me.sibling()
        )
        self.pieces = Exchange(
            OTHERS,
            lambda d: remote(
                self.half.at[piece_of(me.chip_at(d))], self.parts.at[me.chip],
                r.piece_send, r.piece_recv, (number, 0, d), me.chip_after(d),
            ),
        )
        plane = self.planes.at[me.z]
        self.exchange = Exchange(
            3, lambda d: remote(plane, plane, r.plane_send, r.plane_recv, (number, d), me.z_after(d))
        )
        self.total = totals.at[pl.ds(pl.multiple_of(start + me.core * count + me.chip * size, 8), size)]
        self.gathers = Exchange(
            OTHERS,
            lambda d: remote(
                self.total, self.total, r.piece_send, r.piece_recv, (number, 1, d), me.chip_after(d)
            ),
        )
        whole = totals.at[half_of(me.core)]
        self.last = remote(whole, whole, r.half_send, r.half_recv, (number, 1), me.sibling())

    def step(self, number):
        me = self.me
        if number == 0:
            self.halves.start()
        elif number == 1:
            self.halves.wait()
            self.half[...] = self.half[...] + self.mine[...]
            self.parts[me.chip] = self.own_piece[...]
            self.pieces.start()
        elif number == 2:
            self.pieces.wait()
            total = self.parts[0]
            for k in range(1, 16):
                total = total + self.parts[k]
            self.planes[me.z] = total
            self.exchange.start()
        elif number == 3:
            self.exchange.wait()
            self.total[...] = (self.planes[0] + self.planes[1]) + (self.planes[2] + self.planes[3])
            self.gathers.start()
        elif number == 4:
            self.gathers.wait()
            self.last.start()
        else:
            self.last.wait()


def comm_scratch():
    L = LAYERS
    v = pltpu.VMEM
    s = pltpu.SemaphoreType.DMA
    return [
        ("rows_in", v((2, 4, 8, 4, SIDE * D), f32)),
        ("chip_parts", v((4, 16, 8, LANES), f32)),
        ("group_parts", v((4, 8, 8, LANES), f32)),
        ("totals", v((L, GRAD_ROWS, LANES), f32)),
        ("row_own", s((5,))),
        ("row_send", s((4, 4))),
        ("row_recv", s((4, 4))),
        ("chip_send", s((4, 16))),
        ("chip_recv", s((4, 16))),
        ("group_send", s((4, 8))),
        ("group_recv", s((4, 8))),
        ("half_send", s((len(PARCELS), 2))),
        ("half_recv", s((len(PARCELS), 2))),
        ("piece_send", s((len(PARCELS), 2, 16))),
        ("piece_recv", s((len(PARCELS), 2, 16))),
        ("plane_send", s((len(PARCELS), 4))),
        ("plane_recv", s((len(PARCELS), 4))),
        ("member_send", s((len(PARCELS), 8))),
        ("member_recv", s((len(PARCELS), 8))),
        ("out_sem", s((2,))),
        ("param_sem", s((12,))),
    ] + [
        (kind + str(number), v(lead + (PARCELS[number][2] // share, LANES), f32))
        for number in range(len(PARCELS))
        for kind, lead, share in (("half", (), 2), ("parts", (16,), 32), ("planes", (4,), 32))
    ]


def layers_kernel(names, *refs):
    r = SimpleNamespace(**dict(zip(names, refs)))
    me = Place()
    barrier = greet(me)
    own_rows = pltpu.make_async_copy(r.tokens, r.own, r.row_own.at[4])
    loads = [
        pltpu.make_async_copy(getattr(r, name + "_in"), getattr(r, name), r.param_sem.at[k])
        for k, name in enumerate(("sizes",) + PARAMS)
    ]
    loads[0].start()
    own_rows.start()
    for load in loads[1:]:
        load.start()
    mine = pl.ds(me.z * 8, 8)
    tokens_in = RowsIn(r, me, r.tokens, r.rows_in.at[0], 0)
    upstream_in = RowsIn(r, me, r.cotangent, r.rows_in.at[1], 1)
    act_out = RowsOut(r, me, r.rows_in.at[1], r.act.at[mine], 2)
    grad_out = RowsOut(r, me, r.rows_in.at[1], r.rows_in.at[0, me.z], 3)
    sums = [SmallSum(r, me, number) for number in range(4)]
    outer, early, last = (WeightSum(r, me, number) for number in range(3))

    def run(work):
        pl.when(me.z >= 0)(work)

    pl.semaphore_wait(barrier, OTHERS + GROUP)
    tokens_in.start()
    loads[0].wait()
    own_rows.wait()

    @run
    def first_statistics():
        prepare_rows(r, me.z)
        sums[0].put(row_statistics(r))

    sums[0].start()

    @run
    def masks():
        prepare_masks(r, me.z)

    for load in loads[1:]:
        load.wait()

    @run
    def first_weights():
        counted(0, LAYERS, functools.partial(prepare_weights, r))
        r.grads[...] = jnp.zeros_like(r.grads)

    sums[0].step()
    tokens_in.wait()
    upstream_in.start()

    @run
    def tokens():
        take_rows(r.rows_in.at[0], r.x.at[0], r.mask)

    use_statistics(r, 0, sums[0].finish())

    @run
    def first_layer():
        forward_local(r, 0)
        forward_mixer(r, 0)
        forward_rest(r, 0)
        sums[1].put(statistics_partial(r))

    sums[1].start()

    sums[1].step()
    upstream_in.wait()

    @run
    def upstream():
        take_rows(r.rows_in.at[1], r.dy, r.mask)

    use_statistics(r, 1, sums[1].finish())

    @run
    def second_layer():
        forward_local(r, 1)
        forward_mixer(r, 1)
        turn_rest(r, 1)
        give_rows(r.temp, r.rows_in.at[1])

    act_out.start()

    @run
    def second_backward():
        backward_mixer(r, 1)
        backward_local(r, 1)
        sums[2].put(statistics_grad_partial(r, 1))

    sums[2].start()

    @run
    def second_products():
        feed_forward_grads(r, 1)
        mixer_grads(r, 1)

    sums[2].step()

    @run
    def second_local_products():
        local_grads(r, 1)
        vector_grads(r, 1)

    early.step(0)
    use_statistics_grad(r, 1, sums[2].finish())

    @run
    def between():
        backward_input(r, 1)

    early.step(1)

    @run
    def first_backward():
        backward_rest(r, 0)
        backward_mixer(r, 0)
        feed_forward_grads(r, 0)
        mixer_grads(r, 0)

    outer.step(0)
    early.step(2)

    @run
    def first_local_backward():
        backward_local(r, 0)
        sums[3].put(statistics_grad_partial(r, 0))

    sums[3].start()
    outer.step(1)

    @run
    def first_local_products():
        local_grads(r, 0)
        vector_grads(r, 0)

    last.step(0)
    early.step(3)
    act_out.wait()

    @run
    def input_grad():
        partial_input(r, 0)
        give_rows(r.dy, r.rows_in.at[1])

    grad_out.start()
    last.step(1)
    sums[3].step()
    outer.step(2)
    last.step(2)
    early.step(4)
    use_statistics_grad(r, 0, sums[3].finish())
    outer.step(3)
    last.step(3)
    grad_out.wait()

    @run
    def correction():
        corrected_rows(r, r.own)

    copy = pltpu.make_async_copy(r.own, r.grad, r.out_sem.at[0])
    copy.start()
    early.step(5)
    last.step(4)
    outer.step(4)
    last.step(5)
    outer.step(5)
    totals = pltpu.make_async_copy(r.totals, r.grad_sums, r.out_sem.at[1])
    totals.start()
    copy.wait()
    totals.wait()


def unpack_kernel(act_in, grad_in, totals_in, act, grad, *refs):
    count = len(PARAMS)
    outs, parts, (rows, totals, sems) = refs[:count], refs[count : 2 * count], refs[2 * count :]
    loads = [
        pltpu.make_async_copy(src, dst, sems.at[0, k])
        for k, (src, dst) in enumerate(
            ((totals_in.at[0], totals.at[0]), (totals_in.at[1], totals.at[1]), (act_in, rows.at[0]),
             (grad_in, rows.at[1]))
        )
    ]
    stores = [
        pltpu.make_async_copy(src, dst, sems.at[1, k])
        for k, (src, dst) in enumerate(
            ((rows.at[0], act), (rows.at[1], grad)) + tuple(zip(parts, outs))
        )
    ]
    for load in loads:
        load.start()
    gains, biases, depth, spread, first, second, mixer, output, expand, ebias, reduce = parts
    for l in range(LAYERS):
        loads[l].wait()

        def taken(place, count, width=D, start=0):
            return totals[l, place : place + count, start : start + width]

        gains[l] = taken(1216, 4)
        biases[:, l] = taken(1220, 12)
        depth[:, l] = taken(1232, 9)
        spread[l] = taken(1241, 4)
        first[l] = taken(1024, D)
        second[l] = taken(1120, D)
        output[l] = taken(576, D)
        mixer[l, :, 0:D] = taken(768, D)
        mixer[l, :, D : 2 * D] = taken(864, D)
        for t, place in enumerate(VALUE_PLACES):
            mixer[l, :, 2 * D + t * 32 : 2 * D + (t + 1) * 32] = taken(place, D, 32, D)
        for t in range(3):
            at = slice(t * LANES, (t + 1) * LANES)
            expand[l, :, at] = taken(t * D, D, LANES)
            reduce[l, :, at] = taken(288 + t * D, D, LANES)
            ebias[l : l + 1, at] = taken(1245 + t, 1, LANES)
    for store in stores[2:]:
        store.start()
    for load, store in zip(loads[2:], stores[:2]):
        load.wait()
        store.start()
    for store in stores:
        store.wait()


def turned(params):
    gains, biases, depth, spread, *maps, ebias, reduce = params
    return (gains, jnp.swapaxes(biases, 0, 1), jnp.swapaxes(depth, 0, 1), spread, *maps, ebias,
            jnp.swapaxes(reduce, 1, 2))


def shards(tokens, cotangent, image_size, slot_image, slot_batch, *params):
    params = turned(params)
    sizes = image_size.T
    scratch = scratch_list() + comm_scratch()
    scratch += [
        (name, pltpu.VMEM(p.shape, p.dtype)) for name, p in zip(("sizes",) + PARAMS, (sizes,) + params)
    ]
    ins = ("tokens", "cotangent", "slot_image", "slot_batch", "sizes_in")
    ins += tuple(name + "_in" for name in PARAMS)
    outs = ("act", "grad", "grad_sums")
    names = ins + outs + tuple(name for name, _ in scratch)
    anywhere = pl.BlockSpec(memory_space=pl.ANY)
    smem = pl.BlockSpec(memory_space=pltpu.SMEM)
    rows = jax.ShapeDtypeStruct(tokens.shape, f32)
    act, grad, totals = pl.pallas_call(
        functools.partial(layers_kernel, names),
        out_shape=[rows, rows, jax.ShapeDtypeStruct((LAYERS, GRAD_ROWS, LANES), f32)],
        in_specs=[anywhere, anywhere, smem, smem, anywhere] + [anywhere] * len(params),
        out_specs=[anywhere] * 3,
        scratch_shapes=[shape for _, shape in scratch],
        compiler_params=pltpu.CompilerParams(
            collective_id=0, has_side_effects=True, vmem_limit_bytes=63 * 2**20
        ),
        name="layers",
    )(tokens, cotangent, slot_image, slot_batch, sizes, *params)
    act, grad, *grads = pl.pallas_call(
        unpack_kernel,
        out_shape=[rows, rows] + [jax.ShapeDtypeStruct(p.shape, f32) for p in params],
        in_specs=[anywhere] * 3,
        out_specs=[anywhere] * (2 + len(params)),
        scratch_shapes=[pltpu.VMEM(p.shape, f32) for p in params]
        + [
            pltpu.VMEM((2,) + tokens.shape, f32),
            pltpu.VMEM(totals.shape, f32),
            pltpu.SemaphoreType.DMA((2, 2 + len(params))),
        ],
        compiler_params=pltpu.CompilerParams(vmem_limit_bytes=60 * 2**20),
        name="unpack",
    )(act, grad, totals)
    return (act, grad) + turned(grads)


def solution(mesh):
    rows = P("dp", "segment", None)
    return jax.shard_map(
        shards,
        mesh=mesh,
        in_specs=(rows, rows, P(), P("dp"), P("dp")) + (P(),) * len(PARAMS),
        out_specs=(rows, rows) + (P(),) * len(PARAMS),
        check_vma=False,
    )
```

profile of v0, /device:TPU:1, one launch (start us, length us, event | category | flops | bytes accessed | tf_op | source)
XLA Modules:
  0.0 101.1 jit_solution(4604212336588639663)
XLA Ops:
  0.7 97.2 %layers.1 = (f32[32,4,1536]{2,1,0:T(4,128)}, f32[32,4,1536]{2,1,0:T(4,128)}, f32[2,1280,128]{2,1,0:T(8,128)}) custom-call(f32[32,4,1536]{2,1,0:T(4,128)} %refs_0_.1, f32[32,4,1536]{2,1,0:T(4,128)} %refs_1_.1, s32[32]{0:T(128)} %refs_2_.1, s32[32]{0:T(128)} %refs_3_.1, s32[2,1024]{1,0:T(2,128)} %bitcast.10, f32[2,4,96]{2,1,0:T(4,128)} %refs_5_.1, ...), custom_call_target="tpu_custom_call" | custom-call | tf_op jit(solution)/shard_map/layers/pallas_call | solution.py:1350
  97.8 3.1 %unpack.1 = (f32[32,4,1536]{2,1,0:T(4,128)}, f32[32,4,1536]{2,1,0:T(4,128)}, f32[2,4,96]{2,1,0:T(4,128)}, f32[12,2,96]{2,1,0:T(2,128)}, f32[9,2,96]{2,1,0:T(2,12...) custom-call(f32[32,4,1536]{2,1,0:T(4,128)} %get-tuple-element.29.act, ...), custom_call_target="tpu_custom_call" | custom-call | tf_op jit(solution)/shard_map/unpack/pallas_call | solution.py:1361
where the time goes:
time: 101 us
  Pallas kernels  100 us (99%)
    pallas_call x1, Pallas kernels, shards(): pl.pallas_call(functools.partial(layers_kernel, names), out_shape=[rows,...  97.2 us
    pallas_call x1, Pallas kernels, shards(): pl.pallas_call(unpack_kernel, out_shape=[rows, rows] + [jax.ShapeDtypeStr...  3.11 us

commit v1 on v0

--- a/solution.py
+++ b/solution.py
@@ -1153,13 +1153,13 @@
 
     sums[0].step()
     tokens_in.wait()
-    upstream_in.start()
 
     @run
     def tokens():
         take_rows(r.rows_in.at[0], r.x.at[0], r.mask)
 
     use_statistics(r, 0, sums[0].finish())
+    upstream_in.start()
 
     @run
     def first_layer():
@@ -1186,7 +1186,6 @@
         turn_rest(r, 1)
         give_rows(r.temp, r.rows_in.at[1])
 
-    act_out.start()
 
     @run
     def second_backward():
@@ -1202,6 +1201,7 @@
         mixer_grads(r, 1)
 
     sums[2].step()
+    act_out.start()
 
     @run
     def second_local_products():

time: 101 us -> 103 us (1.020)
  Pallas kernels: 100 us -> 102 us
    pallas_call x1, Pallas kernels: 97.2 us -> 98.7 us  [shards(): pl.pallas_call(functools.partial(layers_kernel, names), out_shape=[rows,...]
where the time goes in v1:
time: 103 us
  Pallas kernels  102 us (99%)
    pallas_call x1, Pallas kernels, shards(): pl.pallas_call(functools.partial(layers_kernel, names), out_shape=[rows,...  98.7 us
    pallas_call x1, Pallas kernels, shards(): pl.pallas_call(unpack_kernel, out_shape=[rows, rows] + [jax.ShapeDtypeStr...  3.11 us

profile of v1, /device:TPU:1, one launch (start us, length us, event | category | flops | bytes accessed | tf_op | source)
XLA Modules:
  0.0 102.6 jit_solution(7636143241813804409)
XLA Ops:
  0.7 98.7 %layers.1 = (f32[32,4,1536]{2,1,0:T(4,128)}, f32[32,4,1536]{2,1,0:T(4,128)}, f32[2,1280,128]{2,1,0:T(8,128)}) custom-call(f32[32,4,1536]{2,1,0:T(4,128)} %refs_0_.1, f32[32,4,1536]{2,1,0:T(4,128)} %refs_1_.1, s32[32]{0:T(128)} %refs_2_.1, s32[32]{0:T(128)} %refs_3_.1, s32[2,1024]{1,0:T(2,128)} %bitcast.10, f32[2,4,96]{2,1,0:T(4,128)} %refs_5_.1, ...), custom_call_target="tpu_custom_call" | custom-call | tf_op jit(solution)/shard_map/layers/pallas_call | solution.py:1350
  99.3 3.1 %unpack.1 = (f32[32,4,1536]{2,1,0:T(4,128)}, f32[32,4,1536]{2,1,0:T(4,128)}, f32[2,4,96]{2,1,0:T(4,128)}, f32[12,2,96]{2,1,0:T(2,128)}, f32[9,2,96]{2,1,0:T(2,12...) custom-call(f32[32,4,1536]{2,1,0:T(4,128)} %get-tuple-element.29.act, ...), custom_call_target="tpu_custom_call" | custom-call | tf_op jit(solution)/shard_map/unpack/pallas_call | solution.py:1361
